TPU v7x, 32 devices: a whole 2x2x4 slice. The times are simulated.
32 devices in a mesh: cand: 16 (over z, y, core), head: 2 (over x).
Axes of the slice: x: 2, y: 2, z: 4, core: 2. Of those that a mesh axis runs over, the one named last changes fastest.
Arguments:
- item_feats: bfloat16 [16384, 1024], P('cand', 'head'), may hold values from -6 to 6
- event_feats: bfloat16 [32, 64, 1024], P('cand', None, 'head'), may hold values from -6 to 6
- memory_cache: bfloat16 [32, 8, 128, 128], P('cand', 'head'), may hold values from -36 to 36
- norm_cache: bfloat16 [32, 8, 128], P('cand', 'head'), may hold values from -6 to 6
- query_weight: bfloat16 [1024, 1024], P(None, 'head'), may hold values from -0.1875 to 0.1875
- key_weight: bfloat16 [1024, 1024], P(None, 'head'), may hold values from -0.1875 to 0.1875
- value_weight: bfloat16 [1024, 1024], P(None, 'head'), may hold values from -0.1875 to 0.1875
- gate_weight: bfloat16 [2, 1024, 8], P(None, None, 'head'), may hold values from -0.1875 to 0.1875
- input_bias: float32 [8], P('head'), may hold values from -2 to 2
- forget_bias: float32 [8], P('head'), may hold values from 1 to 7
- head_gain: float32 [8, 128], P('head'), may hold values from 0.4 to 1.6
- tile_list: int32 [32, 4, 2], P('cand'), may hold values from 0 to 127, as said below
Outputs:
- new_memory: bfloat16 [32, 8, 128, 128], P('cand', 'head')
- new_norm: bfloat16 [32, 8, 128], P('cand', 'head')
- scores: float32 [32, 1024], P('cand', 'head')
Inputs may be any that keep to these rules, and one draw needn't show every extreme that they name: `tile_list`: the 2 tiles of a group differ and lie in one block of 8 tiles (the tiles of one index of cand); the groups of a user lie in different blocks. The groups of the users of one index of cand name one block at most 2 times, and some block exactly 2 times. All users' groups name one block at most 16 times, and some block exactly 16 times.
All inputs are finite; a program needn't handle non-finite values.
Results may differ from a plain program's by a relative error of at most 0.0059.
Values may be sent and summed in bfloat16 or wider, within the bound.
A program may use at most 64 MiB of HBM per device.

v0:
```python
import math

import jax
import jax.numpy as jnp
from jax import lax
from jax.sharding import PartitionSpec as P

D = 1024
DH = 128
TILE = 128
TILES_DEV = 8
TPD = 2
GROUPS = 4
CAP = 2


def score_block(query_tiles, item_tiles, head_gain, memory, normalizer, tiles):
    safe = jnp.maximum(tiles, 0)
    count = tiles.shape[0]
    heads_dev = memory.shape[1]
    head_size = memory.shape[2]
    picked = query_tiles[safe].reshape(count, -1, heads_dev, head_size)
    feats = item_tiles[safe].reshape(count, -1, heads_dev, head_size)
    numer = jnp.einsum("schj,shij->schi", picked, memory, preferred_element_type=jnp.float32)
    denom = jnp.einsum("schj,shj->sch", picked, normalizer, preferred_element_type=jnp.float32)
    normed = numer * lax.rsqrt(jnp.mean(numer * numer, axis=-1, keepdims=True) + 1e-05) * head_gain
    normed = normed / jnp.maximum(jnp.abs(denom), 1.0)[..., None]
    return jnp.sum(normed * feats, axis=(2, 3)) / math.sqrt(D)


def score_slots(query_tiles, item_tiles, head_gain, memory, normalizer, tiles):
    count = tiles.shape[0]
    blocks = count // 16
    memory_b = memory.reshape((blocks, 16) + memory.shape[1:])
    normal_b = normalizer.reshape((blocks, 16) + normalizer.shape[1:])
    tiles_b = tiles.reshape((blocks, 16) + tiles.shape[1:])

    def one_block(packed):
        return score_block(query_tiles, item_tiles, head_gain, packed[0], packed[1], packed[2])

    result = lax.map(one_block, (memory_b, normal_b, tiles_b))
    return result.reshape(count, -1)


def on_device(
    item_feats,
    event_feats,
    memory_cache,
    norm_cache,
    query_weight,
    key_weight,
    value_weight,
    gate_weight,
    input_bias,
    forget_bias,
    head_gain,
    tile_list,
):
    n_cand = lax.axis_size("cand")
    users_dev, events, local_width = event_feats.shape
    heads_dev = memory_cache.shape[1]
    head_size = memory_cache.shape[2]
    full_width = query_weight.shape[0]
    gate_cols = jnp.transpose(gate_weight, (1, 0, 2)).reshape(full_width, 2 * heads_dev)
    event_weights = jnp.concatenate([key_weight, value_weight, gate_cols], axis=1)
    piece = lax.all_gather(event_feats, "head", axis=2, tiled=True)
    rows = piece.reshape(-1, piece.shape[2])
    weights = event_weights
    projected = jnp.dot(rows, weights, preferred_element_type=jnp.float32)
    keys = (projected[:, :local_width] / math.sqrt(DH)).reshape(
        users_dev, events, heads_dev, head_size
    )
    values = projected[:, local_width : 2 * local_width].reshape(
        users_dev, events, heads_dev, head_size
    )
    gates = projected[:, 2 * local_width :].reshape(users_dev, events, 2, heads_dev)
    input_gate = jax.nn.sigmoid(gates[:, :, 0, :] + input_bias)
    cum = jnp.cumsum(jax.nn.log_sigmoid(gates[:, :, 1, :] + forget_bias), axis=1)
    weight = input_gate * jnp.exp(cum[:, -1:, :] - cum)
    carry = jnp.exp(cum[:, -1, :])
    update = jnp.einsum(
        "uthi,uthj->uhij", weight[..., None] * values, keys, precision=lax.Precision.HIGHEST
    )
    new_memory = (carry[:, :, None, None] * memory_cache.astype(jnp.float32) + update).astype(
        jnp.bfloat16
    )
    norm_add = jnp.einsum("uth,uthj->uhj", weight, keys, precision=lax.Precision.HIGHEST)
    new_norm = (carry[:, :, None] * norm_cache.astype(jnp.float32) + norm_add).astype(jnp.bfloat16)
    pool_dev = item_feats.shape[0]
    weights = query_weight
    query_acc = jnp.dot(
        lax.all_gather(item_feats, "head", axis=1, tiled=True),
        weights,
        preferred_element_type=jnp.float32,
    )
    query_tiles = (
        (query_acc / math.sqrt(DH))
        .astype(jnp.bfloat16)
        .reshape(pool_dev // TILE, TILE, heads_dev, head_size)
    )
    item_tiles = item_feats.reshape(pool_dev // TILE, TILE, heads_dev, head_size)
    pairs = users_dev * GROUPS
    flat_tiles = tile_list.reshape(pairs, TPD)
    target = flat_tiles[:, 0] // TILES_DEV
    local_tiles = flat_tiles % TILES_DEV
    order_ids = jnp.arange(pairs, dtype=jnp.int32)
    same_target = target[:, None] == target[None, :]
    earlier = order_ids[None, :] < order_ids[:, None]
    rank = jnp.sum((same_target & earlier).astype(jnp.int32), axis=1)
    slot = target * CAP + rank
    slots_all = n_cand * CAP
    pair_memory = jnp.repeat(new_memory, GROUPS, axis=0)
    pair_norm = jnp.repeat(new_norm, GROUPS, axis=0)
    memory_send = (
        jnp.zeros((slots_all, heads_dev, head_size, head_size), jnp.bfloat16)
        .at[slot]
        .set(pair_memory)
    )
    norm_send = jnp.zeros((slots_all, heads_dev, head_size), jnp.bfloat16).at[slot].set(pair_norm)
    tiles_send = jnp.full((slots_all, TPD), -1, jnp.int32).at[slot].set(local_tiles)
    memory_got, norm_got, tiles_got = (
        lax.all_to_all(
            memory_send.reshape(n_cand, CAP, heads_dev, head_size, head_size),
            "cand",
            split_axis=0,
            concat_axis=0,
            tiled=True,
        ),
        lax.all_to_all(
            norm_send.reshape(n_cand, CAP, heads_dev, head_size),
            "cand",
            split_axis=0,
            concat_axis=0,
            tiled=True,
        ),
        lax.all_to_all(
            tiles_send.reshape(n_cand, CAP, TPD), "cand", split_axis=0, concat_axis=0, tiled=True
        ),
    )
    memory_got = memory_got.reshape(slots_all, heads_dev, head_size, head_size)
    norm_got = norm_got.reshape(slots_all, heads_dev, head_size)
    tiles_got = tiles_got.reshape(slots_all, TPD)
    partial_value = score_slots(query_tiles, item_tiles, head_gain, memory_got, norm_got, tiles_got)
    back = lax.all_to_all(
        partial_value.reshape(n_cand, CAP, TPD * TILE),
        "cand",
        split_axis=0,
        concat_axis=0,
        tiled=True,
    )
    back = back.reshape(slots_all, TPD * TILE)
    pair_scores = back[slot].reshape(users_dev, GROUPS * TPD * TILE)
    scores = lax.psum_scatter(pair_scores, "head", scatter_dimension=1, tiled=True)
    return (new_memory, new_norm, scores)


def solution(mesh):
    in_specs = (
        P("cand", "head"),
        P("cand", None, "head"),
        P("cand", "head", None, None),
        P("cand", "head", None),
        P(None, "head"),
        P(None, "head"),
        P(None, "head"),
        P(None, None, "head"),
        P("head"),
        P("head"),
        P("head", None),
        P("cand", None, None),
    )
    out_specs = (P("cand", "head", None, None), P("cand", "head", None), P("cand", "head"))
    return jax.shard_map(
        on_device, mesh=mesh, in_specs=in_specs, out_specs=out_specs, check_vma=False
    )
```

profile of v0, /device:TPU:1, one launch (start us, length us, event | category | flops | bytes accessed | tf_op | source)
XLA Modules:
  0.0 262.8 jit_solution(10502316786610426625)
XLA Ops:
  7.2 0.8 copy.95
  8.1 0.2 convert_reduce_fusion
  8.4 0.6 scatter_custom_fusion.1
  9.0 0.8 copy.98
  9.8 7.3 %all-to-all-start.1 = ((s32[16,2,2]{1,2,0:T(2,128)}), s32[16,2,2]{1,2,0:T(2,128)S(1)}, u32[]{:S(2)}, u32[]{:S(2)}) async-start(s32[16,2,2]{1,2,0:T(2,128)} %copy.98), calls=%async_computation.1 | async-start | bytes 32768 | tf_op jit(solution)/shard_map/all_to_all | solution.py:136
  17.1 0.7 reshape.143
  17.9 0.2 copy.88
  18.0 6.0 %all_gather.6 = bf16[2,64,1024]{2,1,0:T(8,128)(2,1)S(1)} all-gather(bf16[2,64,512]{2,1,0:T(8,128)(2,1)} %param.15), channel_id=1, replica_groups=mesh['cand'=16,'head'=2] {'head'}, dimensions={2}, use_global_device_ids=true | all-gather | bytes 393216 | tf_op jit(solution)/shard_map/all_gather | solution.py:66
  24.0 2.4 convolution_bitcast_fusion
  26.4 0.1 copy.91
  26.6 0.1 reshape.146
  26.8 0.1 copy.118
  26.9 0.1 reduce_window_sum.11
  27.1 0.1 copy.119
  27.2 0.2 broadcast_multiply_fusion
  27.5 0.3 reshape.218
  27.8 0.2 copy.94
  28.0 0.3 fusion.35
  28.4 0.6 broadcast_in_dim.17
  29.1 1.9 scatter_fusion.1
  30.9 6.5 %all-to-all-start.2 = ((bf16[16,2,4,128]{3,2,1,0:T(4,128)(2,1)}), bf16[16,2,4,128]{3,2,1,0:T(4,128)(2,1)S(1)}, u32[]{:S(2)}, u32[]{:S(2)}) async-start(bf16[16,2,4,128]{3,2,1,0:T(4,128)(2,1)} %bitcast.28), calls=%async_computation.2 | async-start | bytes 65536 | tf_op jit(solution)/shard_map/all_to_all | solution.py:129
  37.4 1.0 fusion.18
  38.5 0.7 copy-done.3
  39.2 0.2 broadcast_in_dim.15
  39.4 3.0 %broadcast_in_dim.14 = bf16[32,4,128,128]{3,2,1,0:T(8,128)(2,1)} broadcast(bf16[]{:T(256)} %constant.73.clone.1), dimensions={} | broadcast | bytes 4194306 | tf_op jit(solution)/shard_map/broadcast_in_dim | solution.py:115
  42.4 2.9 %scatter_fusion = bf16[32,4,128,128]{3,2,1,0:T(8,128)(2,1)} fusion(bf16[32,4,128,128]{3,2,1,0:T(8,128)(2,1)} %broadcast_in_dim.14, s32[8]{0:T(128)S(1)} %fusion.31, bf16[8,4,128,128]{3,2,1,0:T(8,128)(2,1)S(1)} %bitcast.129), kind=kCustom, calls=%fused_computation.3 | custom fusion | bytes 3145760 | tf_op jit(solution)/shard_map/scatter | solution.py:117
  45.2 6.2 %all-to-all-start = ((bf16[16,2,4,128,128]{4,3,2,1,0:T(8,128)(2,1)}), bf16[16,2,4,128,128]{4,3,2,1,0:T(8,128)(2,1)}, u32[]{:S(2)}, u32[]{:S(2)}) async-start(bf16[16,2,4,128,128]{4,3,2,1,0:T(8,128)(2,1)} %bitcast.128), calls=%async_computation | async-start | bytes 8388608 | tf_op jit(solution)/shard_map/all_to_all | solution.py:122
  51.4 0.2 all-gather.2.cloned.1.call-start
  51.7 0.5 all-gather.2.cloned.1.call-update
  52.2 1.1 reshape.219
  53.3 1.5 copy.102
  54.8 0.2 copy.112
  55.0 32.7 %all-gather.2.cloned.1.call-done = bf16[1024,1024]{1,0:T(8,128)(2,1)} async-done(((bf16[1024,512]{1,0:T(8,128)(2,1)}), bf16[1024,1024]{1,0:T(8,128)(2,1)}) %all-gather.2.cloned.1.call-update) | async-done | bytes 2097168 | tf_op jit(solution)/shard_map/all_gather | solution.py:92
  87.7 3.8 %multiply_convert_fusion = bf16[1024,512]{1,0:T(8,128)(2,1)} fusion(bf16[1024,1024]{1,0:T(8,128)(2,1)} %all-gather.2.cloned.1.call-done, bf16[1024,512]{1,0:T(8,128)(2,1)S(1)} %copy-done), kind=kOutput, calls=%fused_computation.33 | convolution fusion | flops 1074790400 | bytes 4194304 | tf_op jit(solution)/shard_map/dot_general | solution.py:91
  91.5 1.3 reshape.152
  92.9 36.6 %all-to-all-done = bf16[16,2,4,128,128]{4,3,2,1,0:T(8,128)(2,1)} async-done(((bf16[16,2,4,128,128]{4,3,2,1,0:T(8,128)(2,1)}), bf16[16,2,4,128,128]{4,3,2,1,0:T(8,128)(2,1)}, u32[]{:S(2)}, u32[]{:S(2)}) %all-to-all-start) | async-done | bytes 4194336 | tf_op jit(solution)/shard_map/all_to_all | solution.py:122
  129.5 85.2 %while.10 = (s32[]{:T(128)}, f32[2,16,256]{2,1,0:T(8,128)S(1)}, bf16[2,16,4,128,128]{4,3,2,1,0:T(8,128)(2,1)}, s32[2,16,2]{2,1,0:T(8,128)S(1)}, bf16[8,128,4,128...) while((s32[]{:T(128)}, f32[2,16,256]{2,1,0:T(8,128)S(1)}, ...), condition=%wide.region_8.9_spmd, body=%wide.region_5.8_spmd.sunk | while | flops 555795520 | bytes 124361728 | solution.py:41
  129.5 0.1 reshape.233
  129.6 5.7 %gather_fusion.1 = bf16[32,128,4,128]{3,2,1,0:T(4,128)(2,1)} fusion(bf16[8,128,4,128]{3,2,1,0:T(4,128)(2,1)S(1)} %get-tuple-element.191, s32[1024]{0:T(1024)S(1)} %pad_clamp_fusion.3), kind=kCustom, calls=%fused_computation.clone.1 | custom fusion | bytes 8388736 | tf_op jit(solution)/shard_map/while/body/eval_jaxpr/gather | solution.py:22
  135.3 7.3 %copy.134 = bf16[16,256,4,128]{1,3,2,0:T(8,128)(2,1)} copy(bf16[16,256,4,128]{3,2,1,0:T(4,128)(2,1)} %bitcast.127) | data formatting | bytes 8388608 | tf_op jit(solution)/shard_map/while/body/eval_jaxpr/reshape | solution.py:22
  142.7 2.8 %fusion.56 = f32[16,4,1,256]{3,2,1,0:T(1,128)S(1)} fusion(bf16[16,256,4,128]{1,3,2,0:T(8,128)(2,1)} %copy.134, bf16[16,4,128,1]{2,1,0,3:T(4,128)(2,1)S(1)} %dynamic-slice_bitcast_fusion.2), kind=kOutput, calls=%fused_computation.20.clone.1 | convolution fusion | flops 4194304 | bytes 4276224 | tf_op jit(solution)/shard_map/while/body/eval_jaxpr/schj,shj->sch/dot_general | solution.py:25
  145.5 3.0 %gather_fusion = bf16[32,128,4,128]{3,1,2,0:T(8,128)(2,1)} fusion(bf16[8,128,4,128]{3,1,2,0:T(8,128)(2,1)S(1)} %get-tuple-element.194, s32[1024]{0:T(1024)S(1)} %pad_clamp_fusion.3), kind=kCustom, calls=%fused_computation.1.clone.1 | custom fusion | bytes 8388736 | tf_op jit(solution)/shard_map/while/body/eval_jaxpr/gather | solution.py:23
  148.6 6.5 %copy.132 = f32[32,128,4,128]{3,1,0,2:T(8,128)} copy(bf16[32,128,4,128]{3,1,2,0:T(8,128)(2,1)} %gather_fusion) | data formatting | bytes 12582912 | tf_op jit(solution)/shard_map/while/body/eval_jaxpr/convert_element_type | solution.py:28
  155.1 9.2 %copy.133 = f32[16,256,4,128]{1,3,2,0:T(8,128)} copy(f32[16,256,4,128]{3,1,0,2:T(8,128)} %bitcast.126) | data formatting | bytes 16777216 | tf_op jit(solution)/shard_map/while/body/eval_jaxpr/convert_element_type | solution.py:28
  164.3 4.2 %fusion.55 = (f32[16,256,4]{1,2,0:T(4,128)S(1)}, f32[16,4,128,256]{3,2,1,0:T(8,128)S(1)}) fusion(bf16[16,256,4,128]{1,3,2,0:T(8,128)(2,1)} %copy.134, bf16[2,16,4,128,128]{4,3,2,1,0:T(8,128)(2,1)} %get-tuple-element.189, s32[]{:T(128)S(6)} %copy.140), kind=kOutput, calls=%fused_computation.8.clone.1 | convolution fusion | flops 541048832 | bytes 14745604 | tf_op jit(solution)/shard_map/while/body/eval_jaxpr/schj,shij->schi/dot_general | solution.py:24
  168.6 0.9 copy-done.1
  169.5 2.5 fusion.58
  172.1 0.1 reshape.233
  172.3 5.7 %gather_fusion.1 = bf16[32,128,4,128]{3,2,1,0:T(4,128)(2,1)} fusion(bf16[8,128,4,128]{3,2,1,0:T(4,128)(2,1)S(1)} %get-tuple-element.191, s32[1024]{0:T(1024)S(1)} %pad_clamp_fusion.3), kind=kCustom, calls=%fused_computation.clone.1 | custom fusion | bytes 8388736 | tf_op jit(solution)/shard_map/while/body/eval_jaxpr/gather | solution.py:22
  177.9 7.3 %copy.134 = bf16[16,256,4,128]{1,3,2,0:T(8,128)(2,1)} copy(bf16[16,256,4,128]{3,2,1,0:T(4,128)(2,1)} %bitcast.127) | data formatting | bytes 8388608 | tf_op jit(solution)/shard_map/while/body/eval_jaxpr/reshape | solution.py:22
  185.3 2.8 %fusion.56 = f32[16,4,1,256]{3,2,1,0:T(1,128)S(1)} fusion(bf16[16,256,4,128]{1,3,2,0:T(8,128)(2,1)} %copy.134, bf16[16,4,128,1]{2,1,0,3:T(4,128)(2,1)S(1)} %dynamic-slice_bitcast_fusion.2), kind=kOutput, calls=%fused_computation.20.clone.1 | convolution fusion | flops 4194304 | bytes 4276224 | tf_op jit(solution)/shard_map/while/body/eval_jaxpr/schj,shj->sch/dot_general | solution.py:25
  188.1 3.0 %gather_fusion = bf16[32,128,4,128]{3,1,2,0:T(8,128)(2,1)} fusion(bf16[8,128,4,128]{3,1,2,0:T(8,128)(2,1)S(1)} %get-tuple-element.194, s32[1024]{0:T(1024)S(1)} %pad_clamp_fusion.3), kind=kCustom, calls=%fused_computation.1.clone.1 | custom fusion | bytes 8388736 | tf_op jit(solution)/shard_map/while/body/eval_jaxpr/gather | solution.py:23
  191.2 6.5 %copy.132 = f32[32,128,4,128]{3,1,0,2:T(8,128)} copy(bf16[32,128,4,128]{3,1,2,0:T(8,128)(2,1)} %gather_fusion) | data formatting | bytes 12582912 | tf_op jit(solution)/shard_map/while/body/eval_jaxpr/convert_element_type | solution.py:28
  197.7 9.2 %copy.133 = f32[16,256,4,128]{1,3,2,0:T(8,128)} copy(f32[16,256,4,128]{3,1,0,2:T(8,128)} %bitcast.126) | data formatting | bytes 16777216 | tf_op jit(solution)/shard_map/while/body/eval_jaxpr/convert_element_type | solution.py:28
  206.9 4.2 %fusion.55 = (f32[16,256,4]{1,2,0:T(4,128)S(1)}, f32[16,4,128,256]{3,2,1,0:T(8,128)S(1)}) fusion(bf16[16,256,4,128]{1,3,2,0:T(8,128)(2,1)} %copy.134, bf16[2,16,4,128,128]{4,3,2,1,0:T(8,128)(2,1)} %get-tuple-element.189, s32[]{:T(128)S(6)} %copy.140), kind=kOutput, calls=%fused_computation.8.clone.1 | convolution fusion | flops 541048832 | bytes 14745604 | tf_op jit(solution)/shard_map/while/body/eval_jaxpr/schj,shij->schi/dot_general | solution.py:24
  211.2 0.9 copy-done.1
  212.1 2.5 fusion.58
  214.7 0.6 reshape_reshape.15
  215.3 19.3 %all-to-all-start.3 = ((f32[16,2,256]{2,1,0:T(2,128)}), f32[16,2,256]{2,1,0:T(2,128)S(1)}, u32[]{:S(2)}, u32[]{:S(2)}) async-start(f32[16,2,256]{2,1,0:T(2,128)} %reshape_reshape.15), calls=%async_computation.3 | async-start | bytes 65536 | tf_op jit(solution)/shard_map/all_to_all | solution.py:144
  234.7 5.9 %all-to-all-done.3 = f32[16,2,256]{2,1,0:T(2,128)S(1)} async-done(((f32[16,2,256]{2,1,0:T(2,128)}), f32[16,2,256]{2,1,0:T(2,128)S(1)}, u32[]{:S(2)}, u32[]{:S(2)}) %all-to-all-start.3) | async-done | bytes 32800 | tf_op jit(solution)/shard_map/all_to_all | solution.py:144
  240.5 0.6 gather_fusion.2
  241.1 1.0 copy.115
  242.2 12.1 %reduce-scatter.4.cloned.1.call-done = f32[512,2]{1,0:T(8,128)} async-done(((f32[1024,2]{1,0:T(8,128)}), f32[512,2]{1,0:T(8,128)}) %reduce-scatter.4.cloned.1.call-update) | async-done | bytes 4112
  254.3 1.7 copy.116
  (56 shorter events, 1.0 us)
Async XLA Ops:
  7.2 80.5 %copy-start = (bf16[1024,512]{1,0:T(8,128)(2,1)S(1)}, bf16[1024,512]{1,0:T(8,128)(2,1)}, u32[]{:S(2)}) copy-start(bf16[1024,512]{1,0:T(8,128)(2,1)} %param.18) | copy-start | bytes 3145732
  9.8 21.1 %all-to-all-start.1 = ((s32[16,2,2]{1,2,0:T(2,128)}), s32[16,2,2]{1,2,0:T(2,128)S(1)}, u32[]{:S(2)}, u32[]{:S(2)}) async-start(s32[16,2,2]{1,2,0:T(2,128)} %copy.98), calls=%async_computation.1 | async-start | bytes 32768 | tf_op jit(solution)/shard_map/all_to_all | solution.py:136
  24.0 2.9 %copy-start.8 = (f32[4]{0:T(128)S(1)}, f32[4]{0:T(128)}, u32[]{:S(2)}) copy-start(f32[4]{0:T(128)} %param.23) | copy-start | bytes 52
  24.0 3.2 %copy-start.9 = (f32[4]{0:T(128)S(1)}, f32[4]{0:T(128)}, u32[]{:S(2)}) copy-start(f32[4]{0:T(128)} %param.22) | copy-start | bytes 52
  26.4 2.0 copy-start.7
  26.4 11.1 %copy-start.4 = (bf16[2,4,128,128]{3,2,1,0:T(8,128)(2,1)S(1)}, bf16[2,4,128,128]{3,2,1,0:T(8,128)(2,1)}, u32[]{:S(2)}) copy-start(bf16[2,4,128,128]{3,2,1,0:T(8,128)(2,1)} %param.16) | copy-start | bytes 786436
  28.4 9.0 %copy-start.6 = (bf16[2,4,128]{2,1,0:T(4,128)(2,1)}, bf16[2,4,128]{2,1,0:T(4,128)(2,1)S(1)}, u32[]{:S(2)}) copy-start(bf16[2,4,128]{2,1,0:T(4,128)(2,1)S(1)} %add_convert_fusion) | copy-start | bytes 6148
  30.9 14.3 %all-to-all-start.2 = ((bf16[16,2,4,128]{3,2,1,0:T(4,128)(2,1)}), bf16[16,2,4,128]{3,2,1,0:T(4,128)(2,1)S(1)}, u32[]{:S(2)}, u32[]{:S(2)}) async-start(bf16[16,2,4,128]{3,2,1,0:T(4,128)(2,1)} %bitcast.28), calls=%async_computation.2 | async-start | bytes 65536 | tf_op jit(solution)/shard_map/all_to_all | solution.py:129
  38.5 0.7 copy-start.3
  45.2 6.9 %copy-start.2 = (bf16[1024,512]{1,0:T(8,128)(2,1)S(1)}, bf16[1024,512]{1,0:T(8,128)(2,1)}, u32[]{:S(2)}) copy-start(bf16[1024,512]{1,0:T(8,128)(2,1)} %param.14) | copy-start | bytes 3145732
  45.2 84.3 %all-to-all-start = ((bf16[16,2,4,128,128]{4,3,2,1,0:T(8,128)(2,1)}), bf16[16,2,4,128,128]{4,3,2,1,0:T(8,128)(2,1)}, u32[]{:S(2)}, u32[]{:S(2)}) async-start(bf16[16,2,4,128,128]{4,3,2,1,0:T(8,128)(2,1)} %bitcast.128), calls=%async_computation | async-start | bytes 8388608 | tf_op jit(solution)/shard_map/all_to_all | solution.py:122
  51.4 36.3 %all-gather.2.cloned.1.call-start = ((), (), s32[]{:S(2)}) async-start(), calls=%async_computation.5 | async-start | bytes 3145728 | tf_op jit(solution)/shard_map/all_gather | solution.py:92
  55.0 74.5 %copy-start.5 = (f32[4,128]{1,0:T(4,128)S(1)}, f32[4,128]{1,0:T(4,128)}, u32[]{:S(2)}) copy-start(f32[4,128]{1,0:T(4,128)} %param.24) | copy-start | bytes 6148
  164.3 5.2 %copy-start.1 = (f32[16,256,4,128]{1,3,2,0:T(8,128)S(1)}, f32[16,256,4,128]{1,3,2,0:T(8,128)}, u32[]{:S(2)}) copy-start(f32[16,256,4,128]{1,3,2,0:T(8,128)} %copy.133) | copy-start | bytes 25165828 | tf_op jit(solution)/shard_map/while
  206.9 5.2 %copy-start.1 = (f32[16,256,4,128]{1,3,2,0:T(8,128)S(1)}, f32[16,256,4,128]{1,3,2,0:T(8,128)}, u32[]{:S(2)}) copy-start(f32[16,256,4,128]{1,3,2,0:T(8,128)} %copy.133) | copy-start | bytes 25165828 | tf_op jit(solution)/shard_map/while
  215.3 25.2 %all-to-all-start.3 = ((f32[16,2,256]{2,1,0:T(2,128)}), f32[16,2,256]{2,1,0:T(2,128)S(1)}, u32[]{:S(2)}, u32[]{:S(2)}) async-start(f32[16,2,256]{2,1,0:T(2,128)} %reshape_reshape.15), calls=%async_computation.3 | async-start | bytes 65536 | tf_op jit(solution)/shard_map/all_to_all | solution.py:144
  234.6 19.7 %reduce-scatter.4.cloned.1.call-start = ((), (), s32[]{:S(2)}) async-start(), calls=%async_computation.6 | async-start | bytes 786432
Sparse Core Ops, SparseCore 0:
  53.8 33.8 all-gather.1
  242.3 11.9 reduce-scatter.3
where the time goes:
time: 265 us; the launch traced here: 263 us
  waiting for transfers between devices  87.8 us (33%)
  local copies, waits for them, and re-layouts  87.4 us (33%)
  starting transfers between devices  39.6 us (15%)
  matrix products  21.7 us (8%)
  between operations  14.3 us (5%)
  other arithmetic  5.96 us (2%)
  blocking collectives  5.96 us (2%)
    all_to_all x1, waiting for transfers between devices, on_device(): lax.all_to_all(memory_send.reshape(n_cand, CAP, heads_dev, head_size, hea...  36.6 us
    all_gather x1, waiting for transfers between devices, on_device(): lax.all_gather(item_feats, 'head', axis=1, tiled=True)  32.7 us
    convert_element_type x4, local copies, waits for them, and re-layouts, score_block(): return jnp.sum(normed * feats, axis=(2, 3)) / math.sqrt(D)  31.5 us
    all_to_all x1, starting transfers between devices, on_device(): lax.all_to_all(partial_value.reshape(n_cand, CAP, TPD * TILE), 'cand', sp...  19.3 us
    reshape x2, local copies, waits for them, and re-layouts, score_block(): picked = query_tiles[safe].reshape(count, -1, heads_dev, head_size)  14.7 us
    unnamed x3, waiting for transfers between devices  12.6 us
    gather x2, local copies, waits for them, and re-layouts, score_block(): picked = query_tiles[safe].reshape(count, -1, heads_dev, head_size)  11.3 us
    dot_general x2, matrix products, score_block(): jnp.einsum('schj,shij->schi', picked, memory, preferred_element_type=jnp....  8.48 us
  transfers between devices with their start and end apart: 6, of which 4 were waited for; matrix products, arithmetic and copies ran while one was open for 9% of the time, Pallas kernels for 0%

commit v1 on v0

v1 whole, which is shorter than its diff:
```python
import functools
import math

import jax
import jax.numpy as jnp
from jax import lax
from jax.experimental import pallas as pl
from jax.experimental.pallas import tpu as pltpu
from jax.sharding import PartitionSpec as P

DH = 128
TILE = 128
TILES_DEV = 8
TPD = 2
GROUPS = 4
PAD = 16
HI = lax.Precision.HIGHEST
MESH = pl.DeviceIdType.MESH


def dot(a, b, precision=None):
    return jnp.dot(a, b, preferred_element_type=jnp.float32, precision=precision)


def kernel(
    n_cand, n_head, users, events, heads, full_width,
    ev_ref, item_ref, mem_ref, nrm_ref, wq_ref, wk_ref, wv_ref, gate_ref, bias_ref, gain_ref, tl_ref, own_tl,
    nm_ref, nn_ref, sc_ref,
    ev, feats, wq, wk, wv, blocks, queries, weighted, tl_all, tl_s, scores, got,
    in_sem, ev_send, ev_recv, item_send, item_recv, tl_send, tl_recv, tl_sem,
    send_sem, recv_sem, back_send, back_recv,
):
    me = lax.axis_index("cand")
    head = lax.axis_index("head")
    core = me % 2
    col = (me // 2) % 2
    line = me // 4
    n_line = n_cand // 4
    width = heads * DH
    rows = users * events
    n_tiles = feats.shape[1] // TILE
    part = full_width // n_head
    norm_row = users * heads * DH

    def source(z, y, k):
        return z * 4 + y * 2 + k

    loads = [
        pltpu.make_async_copy(ev_ref, ev.at[head], in_sem.at[0]),
        pltpu.make_async_copy(wk_ref, wk, in_sem.at[1]),
        pltpu.make_async_copy(wv_ref, wv, in_sem.at[2]),
        pltpu.make_async_copy(item_ref, feats.at[head], in_sem.at[3]),
        pltpu.make_async_copy(wq_ref, wq, in_sem.at[4]),
    ]
    for load in loads:
        load.start()

    barrier = pltpu.get_barrier_semaphore()

    def greet(d, carry):
        c, h = d // n_head, d % n_head

        @pl.when(jnp.logical_or(c != me, h != head))
        def _():
            pl.semaphore_signal(barrier, inc=1, device_id=(c, h), device_id_type=MESH)

        return carry

    lax.fori_loop(0, n_cand * n_head, greet, 0)
    pl.semaphore_wait(barrier, n_cand * n_head - 1)

    def ev_copy(off):
        return pltpu.make_async_remote_copy(
            src_ref=ev_ref, dst_ref=ev.at[head], send_sem=ev_send.at[off], recv_sem=ev_recv.at[head],
            device_id=(me, (head + off) % n_head), device_id_type=MESH,
        )

    for off in range(1, n_head):
        ev_copy(off).start()

    def tl_copy(c):
        return pltpu.make_async_remote_copy(
            src_ref=tl_ref, dst_ref=tl_all.at[me], send_sem=tl_send, recv_sem=tl_recv,
            device_id=(c, head), device_id_type=MESH,
        )

    def send_list(off, carry):
        tl_copy((me + off) % n_cand).start()
        return carry

    lax.fori_loop(1, n_cand, send_list, 0)
    pltpu.make_async_copy(tl_ref, tl_all.at[me], tl_recv).start()

    for off in range(1, n_head):
        src = (head + off) % n_head
        pltpu.make_async_copy(ev.at[src], ev.at[src], ev_recv.at[src]).wait()

    def item_copy(off, t):
        at = pl.ds(pl.multiple_of(t * TILE, TILE), TILE)
        return pltpu.make_async_remote_copy(
            src_ref=item_ref.at[at], dst_ref=feats.at[head, at],
            send_sem=item_send.at[off * n_tiles + t], recv_sem=item_recv.at[head * n_tiles + t],
            device_id=(me, (head + off) % n_head), device_id_type=MESH,
        )

    for t in range(n_tiles):
        for off in range(1, n_head):
            item_copy(off, t).start()

    for load in loads[:3]:
        load.wait()
    gates = jnp.zeros((2 * heads, rows), jnp.float32)
    keys = jnp.zeros((rows, width), jnp.float32)
    values = jnp.zeros((rows, width), jnp.float32)
    for hh in range(n_head):
        at = slice(hh * part, (hh + 1) * part)
        x = ev[hh]
        gates += lax.dot_general(
            gate_ref[:, at], x, (((1,), (1,)), ((), ())), preferred_element_type=jnp.float32
        )
        keys += dot(x, wk[at, :])
        values += dot(x, wv[at, :])
    gates += bias_ref[...]
    keys = keys * (1.0 / math.sqrt(DH))
    values_t = values.T
    forget = gates[heads:]
    log_forget = jnp.minimum(forget, 0.0) - jnp.log1p(jnp.exp(-jnp.abs(forget)))
    s_id = lax.broadcasted_iota(jnp.int32, (rows, rows), 0)
    t_id = lax.broadcasted_iota(jnp.int32, (rows, rows), 1)
    later = jnp.where((s_id > t_id) & (s_id // events == t_id // events), 1.0, 0.0)
    weight = jax.nn.sigmoid(gates[:heads]) * jnp.exp(dot(log_forget, later, HI))
    lane_user = lax.broadcasted_iota(jnp.int32, (heads, rows), 1) // events
    norms = []
    for u in range(users):
        mine = lane_user == u
        carry = jnp.exp(jnp.sum(jnp.where(mine, log_forget, 0.0), axis=1, keepdims=True))
        weight_u = jnp.where(mine, weight, 0.0)
        norm_add = dot(weight_u, keys, HI)
        norm_old = nrm_ref[u].astype(jnp.float32)
        for h in range(heads):
            at = slice(h * DH, (h + 1) * DH)
            update = dot(values_t[at, :] * weight_u[h : h + 1, :], keys[:, at], HI)
            new = carry[h : h + 1, :] * mem_ref[u, h].astype(jnp.float32) + update
            r = (u * heads + h) * DH
            blocks[me, r : r + DH, :] = new.astype(jnp.bfloat16)
            norms.append(carry[h : h + 1, :] * norm_old[h : h + 1, :] + norm_add[h : h + 1, at])
    norms.append(jnp.zeros((PAD - users * heads, DH), jnp.float32))
    blocks[me, norm_row : norm_row + PAD, :] = jnp.concatenate(norms, axis=0).astype(jnp.bfloat16)

    def send(src, way, c):
        return pltpu.make_async_remote_copy(
            src_ref=blocks.at[src], dst_ref=blocks.at[src],
            send_sem=send_sem.at[src * 4 + way], recv_sem=recv_sem.at[src],
            device_id=(c, head), device_id_type=MESH,
        )

    up = source(jnp.minimum(line + 1, n_line - 1), col, core)
    down = source(jnp.maximum(line - 1, 0), col, core)
    across = source(line, 1 - col, core)
    twin = source(line, col, 1 - core)

    def each_send(z, act):
        src = source(z, col, core)

        @pl.when((z <= line) & (line + 1 < n_line))
        def _():
            act(send(src, 0, up))

        @pl.when((z >= line) & (line >= 1))
        def _():
            act(send(src, 1, down))

        act(send(src, 2, across))
        act(send(src, 3, twin))

    def start(copy):
        copy.start()

    def arrived(src):
        pltpu.make_async_copy(blocks.at[src], blocks.at[src], recv_sem.at[src]).wait()

    near = jnp.minimum(line, n_line - 1 - line)
    far_sign = jnp.where(line < n_line - 1 - line, 1, -1)

    def order(n):
        paired = line + jnp.where(n % 2 == 1, -1, 1) * ((n + 1) // 2)
        return jnp.where(n <= 2 * near, paired, line + far_sign * (n - near))

    def from_across(n):
        src = source(order(n), 1 - col, core)
        arrived(src)
        send(src, 3, twin).start()

    each_send(line, start)

    for u in range(users):
        for h in range(heads):
            r = (u * heads + h) * DH
            nm_ref[u, h] = blocks[me, r : r + DH, :]
    final_norms = blocks[me, norm_row : norm_row + PAD, :].astype(jnp.float32)
    for u in range(users):
        nn_ref[u] = final_norms[u * heads : (u + 1) * heads, :].astype(jnp.bfloat16)

    loads[3].wait()
    loads[4].wait()

    def features(t, carry):
        at = pl.ds(pl.multiple_of(t * TILE, TILE), TILE)
        x = feats[head, at, :].astype(jnp.float32)
        for h in range(heads):
            c = slice(h * DH, (h + 1) * DH)
            weighted[t, c, :] = (x[:, c] * (gain_ref[h : h + 1, :] * (1.0 / math.sqrt(full_width)))).T
        return carry

    lax.fori_loop(0, n_tiles, features, 0)

    def project(t, carry):
        at = pl.ds(pl.multiple_of(t * TILE, TILE), TILE)
        for off in range(1, n_head):
            src = (head + off) % n_head
            pltpu.make_async_copy(
                feats.at[src, at], feats.at[src, at], item_recv.at[src * n_tiles + t]
            ).wait()
        acc = jnp.zeros((TILE, width), jnp.float32)
        for hh in range(n_head):
            acc += dot(feats[hh, at, :], wq[hh * part : (hh + 1) * part, :])
        acc = acc * (1.0 / math.sqrt(DH))
        for h in range(heads):
            c = slice(h * DH, (h + 1) * DH)
            queries[t, c, :] = acc[:, c].T.astype(jnp.bfloat16)
        return carry

    lax.fori_loop(0, n_tiles // n_line, project, 0)
    for s in range(1, n_line):

        @pl.when(line - s >= 0)
        def _():
            arrived(source(line - s, col, core))
            each_send(line - s, start)

        @pl.when(line + s < n_line)
        def _():
            arrived(source(line + s, col, core))
            each_send(line + s, start)

        from_across(jnp.int32(s - 1))
        lax.fori_loop(s * n_tiles // n_line, (s + 1) * n_tiles // n_line, project, 0)

    pltpu.make_async_copy(tl_all, tl_all, tl_recv).wait()
    to_smem = pltpu.make_async_copy(tl_all, tl_s, tl_sem)
    to_smem.start()
    to_smem.wait()

    def back_copy(src, h):
        return pltpu.make_async_remote_copy(
            src_ref=scores.at[src], dst_ref=got.at[head, me], send_sem=back_send, recv_sem=back_recv,
            device_id=(src, h), device_id_type=MESH,
        )

    def score(j, carry):
        @pl.when(j == 2 * n_line)
        def _():
            from_across(jnp.int32(n_line - 1))

        z = order(j % n_line)
        y = jnp.where(j < 2 * n_line, col, 1 - col)
        other = (j // n_line) % 2
        k = jnp.where(other == 0, core, 1 - core)
        src = source(z, y, k)

        @pl.when(other == 1)
        def _():
            arrived(src)

        norm_block = blocks[src, norm_row : norm_row + PAD, :]
        for u in range(users):
            picks = [jnp.int32(0), jnp.int32(0)]
            for g in range(GROUPS):
                first = tl_s[src, 0, (u * GROUPS + g) * TPD]
                hit = first // TILES_DEV == me
                for p in range(TPD):
                    tile = tl_s[src, 0, (u * GROUPS + g) * TPD + p]
                    picks[p] = jnp.where(hit, tile % TILES_DEV, picks[p])
            totals = [jnp.zeros((1, TILE), jnp.float32) for _ in range(TPD)]
            for h in range(heads):
                r = (u * heads + h) * DH
                left = jnp.concatenate([blocks[src, r : r + DH, :], norm_block], axis=0)
                c = slice(h * DH, (h + 1) * DH)
                for p in range(TPD):
                    product = dot(left, queries[picks[p], c, :])
                    numer = product[:DH]
                    i = DH + u * heads + h
                    denom = product[i : i + 1]
                    square = jnp.sum(numer * numer, axis=0, keepdims=True)
                    value = jnp.sum(numer * weighted[picks[p], c, :], axis=0, keepdims=True)
                    totals[p] += value * lax.rsqrt(square * (1.0 / DH) + 1e-05) / jnp.maximum(
                        jnp.abs(denom), 1.0
                    )
            for p in range(TPD):
                scores[src, u * TPD + p : u * TPD + p + 1, :] = totals[p]
        for h in range(n_head):
            here = (src == me) & (head == h)

            @pl.when(here)
            def _():
                pltpu.make_async_copy(scores.at[src], got.at[head, me], back_recv).start()

            @pl.when(jnp.logical_not(here))
            def _():
                back_copy(src, h).start()

        return carry

    lax.fori_loop(0, n_cand, score, 0)

    pltpu.make_async_copy(got, got, back_recv).wait()
    n_cols = GROUPS * TPD // n_head
    for u in range(users):
        for q in range(n_cols):
            m = head * n_cols + q
            first = own_tl[0, u * GROUPS * TPD + (m // TPD) * TPD]
            block = first // TILES_DEV
            total = jnp.zeros((TPD, TILE), jnp.float32)
            for hh in range(n_head):
                total += got[hh, block][u * TPD : (u + 1) * TPD]
            row = jnp.where(m % TPD == 0, total[0:1], total[1:2])
            sc_ref[u : u + 1, q * TILE : (q + 1) * TILE] = row

    for off in range(1, n_head):
        ev_copy(off).wait_send()

    def item_left(t, carry):
        for off in range(1, n_head):
            item_copy(off, t).wait_send()
        return carry

    lax.fori_loop(0, n_tiles, item_left, 0)
    rest = pl.ds(0, n_cand - 1)
    pltpu.make_async_copy(tl_all.at[rest], tl_all.at[rest], tl_send).wait()

    def left(copy):
        copy.wait_send()

    def blocks_left(z, carry):
        each_send(z, left)
        send(source(z, 1 - col, core), 3, twin).wait_send()
        return carry

    lax.fori_loop(0, n_line, blocks_left, 0)
    for h in range(n_head):
        here = head == h

        @pl.when(here)
        def _():
            pltpu.make_async_copy(scores.at[rest], scores.at[rest], back_send).wait()

        @pl.when(jnp.logical_not(here))
        def _():
            pltpu.make_async_copy(scores, scores, back_send).wait()


def on_device(
    item_feats, event_feats, memory_cache, norm_cache, query_weight, key_weight, value_weight,
    gate_weight, input_bias, forget_bias, head_gain, tile_list,
):
    n_cand = lax.axis_size("cand")
    n_head = lax.axis_size("head")
    users, events, part = event_feats.shape
    heads = memory_cache.shape[1]
    full_width, width = query_weight.shape
    pool = item_feats.shape[0]
    n_tiles = pool // TILE
    rows = users * events
    entries = users * GROUPS * TPD
    gates_t = jnp.transpose(gate_weight, (0, 2, 1)).reshape(2 * heads, full_width)
    bias = jnp.concatenate([input_bias, forget_bias])[:, None]
    tiles = jnp.pad(tile_list.reshape(1, entries), ((0, 0), (0, 128 - entries)))
    block_rows = users * heads * DH + PAD
    score_rows = max(8, users * TPD)
    vmem = pl.BlockSpec(memory_space=pltpu.VMEM)
    smem = pl.BlockSpec(memory_space=pltpu.SMEM)
    any_space = pl.BlockSpec(memory_space=pl.ANY)
    dma = pltpu.SemaphoreType.DMA
    new_memory, new_norm, scores = pl.pallas_call(
        functools.partial(kernel, n_cand, n_head, users, events, heads, full_width),
        out_shape=(
            jax.ShapeDtypeStruct(memory_cache.shape, jnp.bfloat16),
            jax.ShapeDtypeStruct(norm_cache.shape, jnp.bfloat16),
            jax.ShapeDtypeStruct((users, GROUPS * TPD * TILE // n_head), jnp.float32),
        ),
        in_specs=[any_space, any_space, vmem, vmem, any_space, any_space, any_space, vmem, vmem, vmem, vmem, smem],
        out_specs=(vmem, vmem, vmem),
        scratch_shapes=[
            pltpu.VMEM((n_head, rows, part), jnp.bfloat16),
            pltpu.VMEM((n_head, pool, part), jnp.bfloat16),
            pltpu.VMEM((full_width, width), jnp.bfloat16),
            pltpu.VMEM((full_width, width), jnp.bfloat16),
            pltpu.VMEM((full_width, width), jnp.bfloat16),
            pltpu.VMEM((n_cand, block_rows, DH), jnp.bfloat16),
            pltpu.VMEM((n_tiles, width, TILE), jnp.bfloat16),
            pltpu.VMEM((n_tiles, width, TILE), jnp.float32),
            pltpu.VMEM((n_cand, 1, 128), jnp.int32),
            pltpu.SMEM((n_cand, 1, 128), jnp.int32),
            pltpu.VMEM((n_cand, score_rows, TILE), jnp.float32),
            pltpu.VMEM((n_head, n_cand, score_rows, TILE), jnp.float32),
            dma((5,)),
            dma((n_head,)),
            dma((n_head,)),
            dma((n_head * n_tiles,)),
            dma((n_head * n_tiles,)),
            dma,
            dma,
            dma,
            dma((n_cand * 4,)),
            dma((n_cand,)),
            dma,
            dma,
        ],
        compiler_params=pltpu.CompilerParams(
            collective_id=0, has_side_effects=True, vmem_limit_bytes=48 * 1024 * 1024
        ),
    )(
        event_feats.reshape(rows, part), item_feats, memory_cache, norm_cache, query_weight, key_weight,
        value_weight, gates_t, bias, head_gain, tiles, tiles,
    )
    return new_memory, new_norm, scores


def solution(mesh):
    in_specs = (
        P("cand", "head"),
        P("cand", None, "head"),
        P("cand", "head", None, None),
        P("cand", "head", None),
        P(None, "head"),
        P(None, "head"),
        P(None, "head"),
        P(None, None, "head"),
        P("head"),
        P("head"),
        P("head", None),
        P("cand", None, None),
    )
    out_specs = (P("cand", "head", None, None), P("cand", "head", None), P("cand", "head"))
    return jax.shard_map(
        on_device, mesh=mesh, in_specs=in_specs, out_specs=out_specs, check_vma=False
    )
```

time: 265 us -> 62.3 us (0.24)
  waiting for transfers between devices: 87.8 us -> 0 us
  local copies, waits for them, and re-layouts: 87.4 us -> 10.3 us
  Pallas kernels: 0 us -> 50.1 us
  starting transfers between devices: 39.6 us -> 0 us
  matrix products: 21.7 us -> 0 us
  between operations: 14.3 us -> 0.68 us
  blocking collectives: 5.96 us -> 0 us
  other arithmetic: 5.96 us -> 0.75 us
    pallas_call x0 -> x1, Pallas kernels: none -> 50.1 us  [on_device(): pl.pallas_call(functools.partial(kernel, n_cand, n_head, users, events, h...]
    all_to_all x4 -> x0, waiting for transfers between devices: 42.5 us -> none  [the longest x1 36.6 us: on_device(): lax.all_to_all(memory_send.reshape(n_cand, CAP, heads_dev, head_size, hea...]
    all_to_all x4 -> x0, starting transfers between devices: 39.3 us -> none  [the longest x1 19.3 us: on_device(): lax.all_to_all(partial_value.reshape(n_cand, CAP, TPD * TILE), 'cand', sp...]
    all_gather x1 -> x0, waiting for transfers between devices: 32.7 us -> none  [on_device(): lax.all_gather(item_feats, 'head', axis=1, tiled=True)]
    convert_element_type x4 -> x0, local copies, waits for them, and re-layouts: 31.5 us -> none  [score_block(): return jnp.sum(normed * feats, axis=(2, 3)) / math.sqrt(D)]
    dot_general x8 -> x0, matrix products: 21.7 us -> none  [the longest x2 8.48 us: score_block(): jnp.einsum('schj,shij->schi', picked, memory, preferred_element_type=jnp....]
    reshape x14 -> x2, local copies, waits for them, and re-layouts: 19.7 us -> 0.1 us  [the longest x1 0.09 us: on_device(): tiles = jnp.pad(tile_list.reshape(1, entries), ((0, 0), (0, 128 - entries)))]
    gather x5 -> x0, local copies, waits for them, and re-layouts: 18 us -> none  [the longest x2 11.3 us: score_block(): picked = query_tiles[safe].reshape(count, -1, heads_dev, head_size)]
  transfers between devices with their start and end apart: 6 -> 0, of which waited for: 4 -> 0; matrix products, arithmetic and copies ran while one was open for 9% -> 0% of each run, Pallas kernels for 0% -> 0%
where the time goes in v1:
time: 62.3 us; the launch traced here: 61.8 us
  Pallas kernels  50.1 us (80%)
  local copies, waits for them, and re-layouts  10.3 us (17%)
  other arithmetic  0.75 us (1%)
  between operations  0.68 us (1%)
    pallas_call x1, Pallas kernels, on_device(): pl.pallas_call(functools.partial(kernel, n_cand, n_head, users, events, h...  50.1 us
    unnamed x22, local copies, waits for them, and re-layouts  10.1 us

profile of v1, /device:TPU:1, one launch (start us, length us, event | category | flops | bytes accessed | tf_op | source)
XLA Modules:
  0.0 61.8 jit_solution(5321818260427295760)
XLA Ops:
  0.6 0.0 copy-start.8
  0.6 0.8 %maximum_bitcast_fusion = f32[8,1]{0,1:T(1,128)S(1)} fusion(f32[4]{0:T(128)} %param.21, f32[4]{0:T(128)} %param.20), kind=kLoop, calls=%fused_computation | loop fusion | flops 8 | bytes 64 | tf_op jit(solution)/shard_map/broadcast_in_dim | solution.py:376
  1.4 0.1 copy.18.bias_ref
  1.5 0.8 %copy.17 = s32[2,4,2]{2,1,0:T(4,128)S(1)} copy(s32[2,4,2]{1,2,0:T(2,128)} %param.23) | data formatting | bytes 128 | tf_op args[11]
  2.2 0.1 reshape.17
  2.3 0.0 copy-done.8
  2.4 0.0 copy-start.6
  2.4 0.0 copy-start.7
  2.4 0.6 %copy-done.6 = bf16[2,4,128]{2,1,0:T(4,128)(2,1)S(1)} copy-done((bf16[2,4,128]{2,1,0:T(4,128)(2,1)S(1)}, bf16[2,4,128]{2,1,0:T(4,128)(2,1)}, u32[]{:S(2)}) %copy-start.6) | copy-done | bytes 2072
  3.0 0.0 copy-done.7
  3.1 0.0 copy-start
  3.1 1.2 %copy-done = bf16[1024,512]{1,0:T(8,128)(2,1)S(1)} copy-done((bf16[1024,512]{1,0:T(8,128)(2,1)S(1)}, bf16[1024,512]{1,0:T(8,128)(2,1)}, u32[]{:S(2)}) %copy-start) | copy-done | bytes 1048600
  4.3 0.0 copy-start.1
  4.3 1.2 %copy-done.1 = bf16[1024,512]{1,0:T(8,128)(2,1)S(1)} copy-done((bf16[1024,512]{1,0:T(8,128)(2,1)S(1)}, bf16[1024,512]{1,0:T(8,128)(2,1)}, u32[]{:S(2)}) %copy-start.1) | copy-done | bytes 1048600
  5.5 0.0 copy-start.2
  5.5 1.2 %copy-done.2 = bf16[1024,512]{1,0:T(8,128)(2,1)S(1)} copy-done((bf16[1024,512]{1,0:T(8,128)(2,1)S(1)}, bf16[1024,512]{1,0:T(8,128)(2,1)}, u32[]{:S(2)}) %copy-start.2) | copy-done | bytes 1048600
  6.7 0.0 copy-start.3
  6.7 1.2 %copy-done.3 = bf16[1024,512]{1,0:T(8,128)(2,1)S(1)} copy-done((bf16[1024,512]{1,0:T(8,128)(2,1)S(1)}, bf16[1024,512]{1,0:T(8,128)(2,1)}, u32[]{:S(2)}) %copy-start.3) | copy-done | bytes 1048600
  8.0 0.0 copy-start.4
  8.0 0.9 %copy-done.4 = bf16[2,4,128,128]{3,2,1,0:T(8,128)(2,1)S(1)} copy-done((bf16[2,4,128,128]{3,2,1,0:T(8,128)(2,1)S(1)}, bf16[2,4,128,128]{3,2,1,0:T(8,128)(2,1)}, u32[]{:S(2)}) %copy-start.4) | copy-done | bytes 262168
  8.9 0.0 copy-start.5
  8.9 0.9 %copy-done.5 = bf16[2,64,512]{2,1,0:T(8,128)(2,1)S(1)} copy-done((bf16[2,64,512]{2,1,0:T(8,128)(2,1)S(1)}, bf16[2,64,512]{2,1,0:T(8,128)(2,1)}, u32[]{:S(2)}) %copy-start.5) | copy-done | bytes 131096
  9.8 50.1 %shard_map.139 = (bf16[2,4,128,128]{3,2,1,0:T(8,128)(2,1)S(1)}, bf16[2,4,128]{2,1,0:T(4,128)(2,1)S(1)}, f32[2,512]{1,0:T(2,128)S(1)}) custom-call(bf16[128,512]{1,0:T(8,128)(2,1)S(1)} %bitcast.4, bf16[1024,512]{1,0:T(8,128)(2,1)S(1)} %copy-done, bf16[2,4,128,128]{3,2,1,0:T(8,128)(2,1)S(1)} %copy-done.4, bf16[2,4,128]{2,1,0:T(4,128)(2,1)S(1)} %copy-done.6, ...), custom_call_target="tpu_custom_call" | custom-call | tf_op jit(solution)/shard_map/pallas_call | solution.py:384
  60.0 0.7 %copy.22 = bf16[2,4,128,128]{3,2,1,0:T(8,128)(2,1)} copy(bf16[2,4,128,128]{3,2,1,0:T(8,128)(2,1)S(1)} %get-tuple-element.6) | data formatting | bytes 524288
  60.7 0.6 copy.23
  61.2 0.6 copy.24
  (2 shorter events, 0.0 us)
Async XLA Ops:
  0.6 1.7 %copy-start.8 = (bf16[2,1024,4]{1,2,0:T(4,128)(2,1)S(1)}, bf16[2,1024,4]{1,2,0:T(4,128)(2,1)}, u32[]{:S(2)}) copy-start(bf16[2,1024,4]{1,2,0:T(4,128)(2,1)} %param.19) | copy-start | bytes 49156
  2.4 0.7 %copy-start.6 = (bf16[2,4,128]{2,1,0:T(4,128)(2,1)S(1)}, bf16[2,4,128]{2,1,0:T(4,128)(2,1)}, u32[]{:S(2)}) copy-start(bf16[2,4,128]{2,1,0:T(4,128)(2,1)} %nrm_ref.1) | copy-start | bytes 6148
  2.4 0.7 %copy-start.7 = (f32[4,128]{1,0:T(4,128)S(1)}, f32[4,128]{1,0:T(4,128)}, u32[]{:S(2)}) copy-start(f32[4,128]{1,0:T(4,128)} %gain_ref.1) | copy-start | bytes 6148
  3.1 1.2 %copy-start = (bf16[1024,512]{1,0:T(8,128)(2,1)S(1)}, bf16[1024,512]{1,0:T(8,128)(2,1)}, u32[]{:S(2)}) copy-start(bf16[1024,512]{1,0:T(8,128)(2,1)} %item_ref.1) | copy-start | bytes 3145732
  4.3 1.2 %copy-start.1 = (bf16[1024,512]{1,0:T(8,128)(2,1)S(1)}, bf16[1024,512]{1,0:T(8,128)(2,1)}, u32[]{:S(2)}) copy-start(bf16[1024,512]{1,0:T(8,128)(2,1)} %wq_ref.1) | copy-start | bytes 3145732
  5.5 1.2 %copy-start.2 = (bf16[1024,512]{1,0:T(8,128)(2,1)S(1)}, bf16[1024,512]{1,0:T(8,128)(2,1)}, u32[]{:S(2)}) copy-start(bf16[1024,512]{1,0:T(8,128)(2,1)} %wk_ref.1) | copy-start | bytes 3145732
  6.7 1.2 %copy-start.3 = (bf16[1024,512]{1,0:T(8,128)(2,1)S(1)}, bf16[1024,512]{1,0:T(8,128)(2,1)}, u32[]{:S(2)}) copy-start(bf16[1024,512]{1,0:T(8,128)(2,1)} %wv_ref.1) | copy-start | bytes 3145732
  8.0 0.9 %copy-start.4 = (bf16[2,4,128,128]{3,2,1,0:T(8,128)(2,1)S(1)}, bf16[2,4,128,128]{3,2,1,0:T(8,128)(2,1)}, u32[]{:S(2)}) copy-start(bf16[2,4,128,128]{3,2,1,0:T(8,128)(2,1)} %mem_ref.1) | copy-start | bytes 786436
  8.9 0.9 %copy-start.5 = (bf16[2,64,512]{2,1,0:T(8,128)(2,1)S(1)}, bf16[2,64,512]{2,1,0:T(8,128)(2,1)}, u32[]{:S(2)}) copy-start(bf16[2,64,512]{2,1,0:T(8,128)(2,1)} %param.13) | copy-start | bytes 393220

commit v2 on v1

--- a/solution.py
+++ b/solution.py
@@ -24,9 +24,9 @@
 
 def kernel(
     n_cand, n_head, users, events, heads, full_width,
-    ev_ref, item_ref, mem_ref, nrm_ref, wq_ref, wk_ref, wv_ref, gate_ref, bias_ref, gain_ref, tl_ref, own_tl,
+    ev_ref, item_ref, mem_ref, nrm_ref, wq_ref, wk_ref, wv_ref, gate_ref, bias_i, bias_f, gain_ref, own_tl,
     nm_ref, nn_ref, sc_ref,
-    ev, feats, wq, wk, wv, blocks, queries, weighted, tl_all, tl_s, scores, got,
+    ev, feats, wq, wk, wv, blocks, queries, weighted, tl_ref, tl_all, tl_s, scores, got,
     in_sem, ev_send, ev_recv, item_send, item_recv, tl_send, tl_recv, tl_sem,
     send_sem, recv_sem, back_send, back_recv,
 ):
@@ -55,6 +55,14 @@
     for load in loads:
         load.start()
 
+    entry = lax.broadcasted_iota(jnp.int32, (1, 128), 1)
+    own_row = jnp.zeros((1, 128), jnp.int32)
+    for u in range(users):
+        for g in range(GROUPS):
+            for p in range(TPD):
+                own_row = jnp.where(entry == (u * GROUPS + g) * TPD + p, own_tl[u, p, g], own_row)
+    tl_ref[...] = own_row
+
     barrier = pltpu.get_barrier_semaphore()
 
     def greet(d, carry):
@@ -77,23 +85,6 @@
 
     for off in range(1, n_head):
         ev_copy(off).start()
-
-    def tl_copy(c):
-        return pltpu.make_async_remote_copy(
-            src_ref=tl_ref, dst_ref=tl_all.at[me], send_sem=tl_send, recv_sem=tl_recv,
-            device_id=(c, head), device_id_type=MESH,
-        )
-
-    def send_list(off, carry):
-        tl_copy((me + off) % n_cand).start()
-        return carry
-
-    lax.fori_loop(1, n_cand, send_list, 0)
-    pltpu.make_async_copy(tl_ref, tl_all.at[me], tl_recv).start()
-
-    for off in range(1, n_head):
-        src = (head + off) % n_head
-        pltpu.make_async_copy(ev.at[src], ev.at[src], ev_recv.at[src]).wait()
 
     def item_copy(off, t):
         at = pl.ds(pl.multiple_of(t * TILE, TILE), TILE)
@@ -107,28 +98,51 @@
         for off in range(1, n_head):
             item_copy(off, t).start()
 
+    def tl_copy(c):
+        return pltpu.make_async_remote_copy(
+            src_ref=tl_ref, dst_ref=tl_all.at[me], send_sem=tl_send, recv_sem=tl_recv,
+            device_id=(c, head), device_id_type=MESH,
+        )
+
+    def send_list(off, carry):
+        tl_copy((me + off) % n_cand).start()
+        return carry
+
+    lax.fori_loop(1, n_cand, send_list, 0)
+    pltpu.make_async_copy(tl_ref, tl_all.at[me], tl_recv).start()
+
+    for off in range(1, n_head):
+        src = (head + off) % n_head
+        pltpu.make_async_copy(ev.at[src], ev.at[src], ev_recv.at[src]).wait()
+
     for load in loads[:3]:
         load.wait()
-    gates = jnp.zeros((2 * heads, rows), jnp.float32)
+    pre = []
+    for bias in (bias_i, bias_f):
+        h_id = lax.broadcasted_iota(jnp.int32, (heads, rows), 0)
+        column = jnp.zeros((heads, rows), jnp.float32)
+        for h in range(heads):
+            column = jnp.where(h_id == h, bias[h], column)
+        pre.append(column)
     keys = jnp.zeros((rows, width), jnp.float32)
     values = jnp.zeros((rows, width), jnp.float32)
     for hh in range(n_head):
         at = slice(hh * part, (hh + 1) * part)
         x = ev[hh]
-        gates += lax.dot_general(
-            gate_ref[:, at], x, (((1,), (1,)), ((), ())), preferred_element_type=jnp.float32
-        )
+        for i in range(2):
+            pre[i] += lax.dot_general(
+                gate_ref[i, :, at], x, (((1,), (1,)), ((), ())), preferred_element_type=jnp.float32
+            )
         keys += dot(x, wk[at, :])
         values += dot(x, wv[at, :])
-    gates += bias_ref[...]
     keys = keys * (1.0 / math.sqrt(DH))
     values_t = values.T
-    forget = gates[heads:]
+    forget = pre[1]
     log_forget = jnp.minimum(forget, 0.0) - jnp.log1p(jnp.exp(-jnp.abs(forget)))
     s_id = lax.broadcasted_iota(jnp.int32, (rows, rows), 0)
     t_id = lax.broadcasted_iota(jnp.int32, (rows, rows), 1)
     later = jnp.where((s_id > t_id) & (s_id // events == t_id // events), 1.0, 0.0)
-    weight = jax.nn.sigmoid(gates[:heads]) * jnp.exp(dot(log_forget, later, HI))
+    weight = jax.nn.sigmoid(pre[0]) * jnp.exp(dot(log_forget, later, HI))
     lane_user = lax.broadcasted_iota(jnp.int32, (heads, rows), 1) // events
     norms = []
     for u in range(users):
@@ -318,7 +332,7 @@
     for u in range(users):
         for q in range(n_cols):
             m = head * n_cols + q
-            first = own_tl[0, u * GROUPS * TPD + (m // TPD) * TPD]
+            first = own_tl[u, 0, m // TPD]
             block = first // TILES_DEV
             total = jnp.zeros((TPD, TILE), jnp.float32)
             for hh in range(n_head):
@@ -371,15 +385,13 @@
     pool = item_feats.shape[0]
     n_tiles = pool // TILE
     rows = users * events
-    entries = users * GROUPS * TPD
-    gates_t = jnp.transpose(gate_weight, (0, 2, 1)).reshape(2 * heads, full_width)
-    bias = jnp.concatenate([input_bias, forget_bias])[:, None]
-    tiles = jnp.pad(tile_list.reshape(1, entries), ((0, 0), (0, 128 - entries)))
+    gates_t = jnp.transpose(gate_weight, (0, 2, 1))
+    tiles = jnp.transpose(tile_list, (0, 2, 1))
     block_rows = users * heads * DH + PAD
     score_rows = max(8, users * TPD)
     vmem = pl.BlockSpec(memory_space=pltpu.VMEM)
     smem = pl.BlockSpec(memory_space=pltpu.SMEM)
-    any_space = pl.BlockSpec(memory_space=pl.ANY)
+    any_space = pl.BlockSpec(memory_space=pltpu.HBM)
     dma = pltpu.SemaphoreType.DMA
     new_memory, new_norm, scores = pl.pallas_call(
         functools.partial(kernel, n_cand, n_head, users, events, heads, full_width),
@@ -388,7 +400,7 @@
             jax.ShapeDtypeStruct(norm_cache.shape, jnp.bfloat16),
             jax.ShapeDtypeStruct((users, GROUPS * TPD * TILE // n_head), jnp.float32),
         ),
-        in_specs=[any_space, any_space, vmem, vmem, any_space, any_space, any_space, vmem, vmem, vmem, vmem, smem],
+        in_specs=[any_space, any_space, vmem, vmem, any_space, any_space, any_space, vmem, smem, smem, vmem, smem],
         out_specs=(vmem, vmem, vmem),
         scratch_shapes=[
             pltpu.VMEM((n_head, rows, part), jnp.bfloat16),
@@ -399,6 +411,7 @@
             pltpu.VMEM((n_cand, block_rows, DH), jnp.bfloat16),
             pltpu.VMEM((n_tiles, width, TILE), jnp.bfloat16),
             pltpu.VMEM((n_tiles, width, TILE), jnp.float32),
+            pltpu.VMEM((1, 128), jnp.int32),
             pltpu.VMEM((n_cand, 1, 128), jnp.int32),
             pltpu.SMEM((n_cand, 1, 128), jnp.int32),
             pltpu.VMEM((n_cand, score_rows, TILE), jnp.float32),
@@ -417,11 +430,11 @@
             dma,
         ],
         compiler_params=pltpu.CompilerParams(
-            collective_id=0, has_side_effects=True, vmem_limit_bytes=48 * 1024 * 1024
+            collective_id=0, has_side_effects=True, vmem_limit_bytes=60 * 1024 * 1024
         ),
     )(
         event_feats.reshape(rows, part), item_feats, memory_cache, norm_cache, query_weight, key_weight,
-        value_weight, gates_t, bias, head_gain, tiles, tiles,
+        value_weight, gates_t, input_bias, forget_bias, head_gain, tiles,
     )
     return new_memory, new_norm, scores
 

time: 62.3 us -> 54.8 us (0.88)
  local copies, waits for them, and re-layouts: 10.3 us -> 2.95 us
  Pallas kernels: 50.1 us -> 51 us
  other arithmetic: 0.75 us -> 0 us
    unnamed x22 -> x7, local copies, waits for them, and re-layouts: 10.1 us -> 2.95 us
    pallas_call x1, Pallas kernels: 50.1 us -> 51 us  [on_device(): pl.pallas_call(functools.partial(kernel, n_cand, n_head, users, events, h...]
    broadcast_in_dim x1 -> x0, other arithmetic: 0.75 us -> none  [on_device(): bias = jnp.concatenate([input_bias, forget_bias])[:, None]]
where the time goes in v2:
time: 54.8 us; the launch traced here: 54.6 us
  Pallas kernels  51 us (93%)
  local copies, waits for them, and re-layouts  2.95 us (5%)
  between operations  0.65 us (1%)
    pallas_call x1, Pallas kernels, on_device(): pl.pallas_call(functools.partial(kernel, n_cand, n_head, users, events, h...  51 us
    unnamed x7, local copies, waits for them, and re-layouts  2.95 us

profile of v2, /device:TPU:1, one launch (start us, length us, event | category | flops | bytes accessed | tf_op | source)
XLA Modules:
  0.0 54.6 jit_solution(1006973555304925143)
XLA Ops:
  0.6 51.0 %shard_map.139 = (bf16[2,4,128,128]{3,2,1,0:T(8,128)(2,1)}, bf16[2,4,128]{2,1,0:T(4,128)(2,1)}, f32[2,512]{1,0:T(2,128)}) custom-call(bf16[128,512]{1,0:T(8,128)(2,1)} %bitcast.3, bf16[1024,512]{1,0:T(8,128)(2,1)} %item_ref.1, bf16[2,4,128,128]{3,2,1,0:T(8,128)(2,1)} %mem_ref.1, bf16[2,4,128]{2,1,0:T(4,128)(2,1)} %nrm_ref.1, bf16[1024,512]{1,0:T(8,128)(2,1)} %wq_ref.1, ...), custom_call_target="tpu_custom_call" | custom-call | tf_op jit(solution)/shard_map/pallas_call | solution.py:396
  51.7 0.0 copy-start.1
  51.7 1.7 %copy.18 = bf16[2,4,128,128]{3,2,1,0:T(8,128)(2,1)} copy(bf16[2,4,128,128]{3,2,1,0:T(8,128)(2,1)} %get-tuple-element.6) | data formatting | bytes 524288
  53.3 0.0 copy-done.1
  53.3 0.0 copy-start
  53.4 0.6 %copy.19 = bf16[2,4,128]{2,1,0:T(4,128)(2,1)} copy(bf16[2,4,128]{2,1,0:T(4,128)(2,1)S(1)} %copy-done.1) | data formatting | bytes 4096
  53.9 0.1 copy-done
  54.0 0.6 %copy.20 = f32[2,512]{1,0:T(2,128)} copy(f32[2,512]{1,0:T(2,128)S(1)} %copy-done) | data formatting | bytes 8192
Async XLA Ops:
  51.7 1.7 %copy-start.1 = (bf16[2,4,128]{2,1,0:T(4,128)(2,1)S(1)}, bf16[2,4,128]{2,1,0:T(4,128)(2,1)}, u32[]{:S(2)}) copy-start(bf16[2,4,128]{2,1,0:T(4,128)(2,1)} %get-tuple-element.7) | copy-start | bytes 6148
  53.3 0.7 %copy-start = (f32[2,512]{1,0:T(2,128)S(1)}, f32[2,512]{1,0:T(2,128)}, u32[]{:S(2)}) copy-start(f32[2,512]{1,0:T(2,128)} %get-tuple-element.8) | copy-start | bytes 12292

commit v3 on v2

--- a/solution.py
+++ b/solution.py
@@ -13,7 +13,8 @@
 TILES_DEV = 8
 TPD = 2
 GROUPS = 4
-PAD = 16
+PAD = 32
+PIECES = 2
 HI = lax.Precision.HIGHEST
 MESH = pl.DeviceIdType.MESH
 
@@ -65,16 +66,14 @@
 
     barrier = pltpu.get_barrier_semaphore()
 
-    def greet(d, carry):
-        c, h = d // n_head, d % n_head
-
-        @pl.when(jnp.logical_or(c != me, h != head))
-        def _():
-            pl.semaphore_signal(barrier, inc=1, device_id=(c, h), device_id_type=MESH)
-
-        return carry
-
-    lax.fori_loop(0, n_cand * n_head, greet, 0)
+    def greet(off, carry):
+        d = (me * n_head + head + off) % (n_cand * n_head)
+        pl.semaphore_signal(
+            barrier, inc=1, device_id=(d // n_head, d % n_head), device_id_type=MESH
+        )
+        return carry
+
+    lax.fori_loop(1, n_cand * n_head, greet, 0)
     pl.semaphore_wait(barrier, n_cand * n_head - 1)
 
     def ev_copy(off):
@@ -161,10 +160,13 @@
     norms.append(jnp.zeros((PAD - users * heads, DH), jnp.float32))
     blocks[me, norm_row : norm_row + PAD, :] = jnp.concatenate(norms, axis=0).astype(jnp.bfloat16)
 
-    def send(src, way, c):
+    piece_rows = blocks.shape[1] // PIECES
+
+    def send(src, q, way, c):
+        at = pl.ds(q * piece_rows, piece_rows)
         return pltpu.make_async_remote_copy(
-            src_ref=blocks.at[src], dst_ref=blocks.at[src],
-            send_sem=send_sem.at[src * 4 + way], recv_sem=recv_sem.at[src],
+            src_ref=blocks.at[src, at], dst_ref=blocks.at[src, at],
+            send_sem=send_sem.at[(src * PIECES + q) * 4 + way], recv_sem=recv_sem.at[src * PIECES + q],
             device_id=(c, head), device_id_type=MESH,
         )
 
@@ -173,25 +175,28 @@
     across = source(line, 1 - col, core)
     twin = source(line, col, 1 - core)
 
-    def each_send(z, act):
+    def each_send(z, q, act):
         src = source(z, col, core)
+        act(send(src, q, 2, across))
 
         @pl.when((z <= line) & (line + 1 < n_line))
         def _():
-            act(send(src, 0, up))
+            act(send(src, q, 0, up))
 
         @pl.when((z >= line) & (line >= 1))
         def _():
-            act(send(src, 1, down))
-
-        act(send(src, 2, across))
-        act(send(src, 3, twin))
+            act(send(src, q, 1, down))
+
+        act(send(src, q, 3, twin))
 
     def start(copy):
         copy.start()
 
-    def arrived(src):
-        pltpu.make_async_copy(blocks.at[src], blocks.at[src], recv_sem.at[src]).wait()
+    def arrived(src, q):
+        at = pl.ds(q * piece_rows, piece_rows)
+        pltpu.make_async_copy(
+            blocks.at[src, at], blocks.at[src, at], recv_sem.at[src * PIECES + q]
+        ).wait()
 
     near = jnp.minimum(line, n_line - 1 - line)
     far_sign = jnp.where(line < n_line - 1 - line, 1, -1)
@@ -200,12 +205,13 @@
         paired = line + jnp.where(n % 2 == 1, -1, 1) * ((n + 1) // 2)
         return jnp.where(n <= 2 * near, paired, line + far_sign * (n - near))
 
-    def from_across(n):
+    def from_across(n, q):
         src = source(order(n), 1 - col, core)
-        arrived(src)
-        send(src, 3, twin).start()
-
-    each_send(line, start)
+        arrived(src, q)
+        send(src, q, 3, twin).start()
+
+    for q in range(PIECES):
+        each_send(line, q, start)
 
     for u in range(users):
         for h in range(heads):
@@ -247,17 +253,19 @@
     lax.fori_loop(0, n_tiles // n_line, project, 0)
     for s in range(1, n_line):
 
-        @pl.when(line - s >= 0)
-        def _():
-            arrived(source(line - s, col, core))
-            each_send(line - s, start)
-
-        @pl.when(line + s < n_line)
-        def _():
-            arrived(source(line + s, col, core))
-            each_send(line + s, start)
-
-        from_across(jnp.int32(s - 1))
+        for q in range(PIECES):
+
+            @pl.when(line - s >= 0)
+            def _():
+                arrived(source(line - s, col, core), q)
+                each_send(line - s, q, start)
+
+            @pl.when(line + s < n_line)
+            def _():
+                arrived(source(line + s, col, core), q)
+                each_send(line + s, q, start)
+
+            from_across(jnp.int32(s - 1), q)
         lax.fori_loop(s * n_tiles // n_line, (s + 1) * n_tiles // n_line, project, 0)
 
     pltpu.make_async_copy(tl_all, tl_all, tl_recv).wait()
@@ -274,7 +282,8 @@
     def score(j, carry):
         @pl.when(j == 2 * n_line)
         def _():
-            from_across(jnp.int32(n_line - 1))
+            for q in range(PIECES):
+                from_across(jnp.int32(n_line - 1), q)
 
         z = order(j % n_line)
         y = jnp.where(j < 2 * n_line, col, 1 - col)
@@ -284,9 +293,10 @@
 
         @pl.when(other == 1)
         def _():
-            arrived(src)
-
-        norm_block = blocks[src, norm_row : norm_row + PAD, :]
+            for q in range(PIECES):
+                arrived(src, q)
+
+        norm_block = blocks[src, norm_row : norm_row + PAD // 2, :]
         for u in range(users):
             picks = [jnp.int32(0), jnp.int32(0)]
             for g in range(GROUPS):
@@ -356,8 +366,9 @@
         copy.wait_send()
 
     def blocks_left(z, carry):
-        each_send(z, left)
-        send(source(z, 1 - col, core), 3, twin).wait_send()
+        for q in range(PIECES):
+            each_send(z, q, left)
+            send(source(z, 1 - col, core), q, 3, twin).wait_send()
         return carry
 
     lax.fori_loop(0, n_line, blocks_left, 0)
@@ -424,8 +435,8 @@
             dma,
             dma,
             dma,
-            dma((n_cand * 4,)),
-            dma((n_cand,)),
+            dma((n_cand * PIECES * 4,)),
+            dma((n_cand * PIECES,)),
             dma,
             dma,
         ],

time: 54.8 us -> 54.8 us (level)
  no operation moved by 1% of the time
where the time goes in v3:
time: 54.8 us; the launch traced here: 54.6 us
  Pallas kernels  51 us (93%)
  local copies, waits for them, and re-layouts  2.95 us (5%)
  between operations  0.65 us (1%)
    pallas_call x1, Pallas kernels, on_device(): pl.pallas_call(functools.partial(kernel, n_cand, n_head, users, events, h...  51 us
    unnamed x7, local copies, waits for them, and re-layouts  2.95 us

profile of v3, /device:TPU:1, one launch (start us, length us, event | category | flops | bytes accessed | tf_op | source)
XLA Modules:
  0.0 54.6 jit_solution(4735168629165098791)
XLA Ops:
  0.6 51.0 %shard_map.139 = (bf16[2,4,128,128]{3,2,1,0:T(8,128)(2,1)}, bf16[2,4,128]{2,1,0:T(4,128)(2,1)}, f32[2,512]{1,0:T(2,128)}) custom-call(bf16[128,512]{1,0:T(8,128)(2,1)} %bitcast.3, bf16[1024,512]{1,0:T(8,128)(2,1)} %item_ref.1, bf16[2,4,128,128]{3,2,1,0:T(8,128)(2,1)} %mem_ref.1, bf16[2,4,128]{2,1,0:T(4,128)(2,1)} %nrm_ref.1, bf16[1024,512]{1,0:T(8,128)(2,1)} %wq_ref.1, ...), custom_call_target="tpu_custom_call" | custom-call | tf_op jit(solution)/shard_map/pallas_call | solution.py:407
  51.7 0.0 copy-start.1
  51.7 1.7 %copy.18 = bf16[2,4,128,128]{3,2,1,0:T(8,128)(2,1)} copy(bf16[2,4,128,128]{3,2,1,0:T(8,128)(2,1)} %get-tuple-element.6) | data formatting | bytes 524288
  53.3 0.0 copy-done.1
  53.3 0.0 copy-start
  53.3 0.6 %copy.19 = bf16[2,4,128]{2,1,0:T(4,128)(2,1)} copy(bf16[2,4,128]{2,1,0:T(4,128)(2,1)S(1)} %copy-done.1) | data formatting | bytes 4096
  53.9 0.1 copy-done
  54.0 0.6 %copy.20 = f32[2,512]{1,0:T(2,128)} copy(f32[2,512]{1,0:T(2,128)S(1)} %copy-done) | data formatting | bytes 8192
Async XLA Ops:
  51.7 1.7 %copy-start.1 = (bf16[2,4,128]{2,1,0:T(4,128)(2,1)S(1)}, bf16[2,4,128]{2,1,0:T(4,128)(2,1)}, u32[]{:S(2)}) copy-start(bf16[2,4,128]{2,1,0:T(4,128)(2,1)} %get-tuple-element.7) | copy-start | bytes 6148
  53.3 0.7 %copy-start = (f32[2,512]{1,0:T(2,128)S(1)}, f32[2,512]{1,0:T(2,128)}, u32[]{:S(2)}) copy-start(f32[2,512]{1,0:T(2,128)} %get-tuple-element.8) | copy-start | bytes 12292

commit v4 on v3

--- a/solution.py
+++ b/solution.py
@@ -74,45 +74,6 @@
         return carry
 
     lax.fori_loop(1, n_cand * n_head, greet, 0)
-    pl.semaphore_wait(barrier, n_cand * n_head - 1)
-
-    def ev_copy(off):
-        return pltpu.make_async_remote_copy(
-            src_ref=ev_ref, dst_ref=ev.at[head], send_sem=ev_send.at[off], recv_sem=ev_recv.at[head],
-            device_id=(me, (head + off) % n_head), device_id_type=MESH,
-        )
-
-    for off in range(1, n_head):
-        ev_copy(off).start()
-
-    def item_copy(off, t):
-        at = pl.ds(pl.multiple_of(t * TILE, TILE), TILE)
-        return pltpu.make_async_remote_copy(
-            src_ref=item_ref.at[at], dst_ref=feats.at[head, at],
-            send_sem=item_send.at[off * n_tiles + t], recv_sem=item_recv.at[head * n_tiles + t],
-            device_id=(me, (head + off) % n_head), device_id_type=MESH,
-        )
-
-    for t in range(n_tiles):
-        for off in range(1, n_head):
-            item_copy(off, t).start()
-
-    def tl_copy(c):
-        return pltpu.make_async_remote_copy(
-            src_ref=tl_ref, dst_ref=tl_all.at[me], send_sem=tl_send, recv_sem=tl_recv,
-            device_id=(c, head), device_id_type=MESH,
-        )
-
-    def send_list(off, carry):
-        tl_copy((me + off) % n_cand).start()
-        return carry
-
-    lax.fori_loop(1, n_cand, send_list, 0)
-    pltpu.make_async_copy(tl_ref, tl_all.at[me], tl_recv).start()
-
-    for off in range(1, n_head):
-        src = (head + off) % n_head
-        pltpu.make_async_copy(ev.at[src], ev.at[src], ev_recv.at[src]).wait()
 
     for load in loads[:3]:
         load.wait()
@@ -123,17 +84,62 @@
         for h in range(heads):
             column = jnp.where(h_id == h, bias[h], column)
         pre.append(column)
-    keys = jnp.zeros((rows, width), jnp.float32)
-    values = jnp.zeros((rows, width), jnp.float32)
-    for hh in range(n_head):
-        at = slice(hh * part, (hh + 1) * part)
-        x = ev[hh]
+    sums = [pre, jnp.zeros((rows, width), jnp.float32), jnp.zeros((rows, width), jnp.float32)]
+
+    def add_half(src):
+        at = pl.ds(pl.multiple_of(src * part, 128), part)
+        x = ev[src]
         for i in range(2):
-            pre[i] += lax.dot_general(
+            sums[0][i] += lax.dot_general(
                 gate_ref[i, :, at], x, (((1,), (1,)), ((), ())), preferred_element_type=jnp.float32
             )
-        keys += dot(x, wk[at, :])
-        values += dot(x, wv[at, :])
+        sums[1] += dot(x, wk[at, :])
+        sums[2] += dot(x, wv[at, :])
+
+    add_half(head)
+    pl.semaphore_wait(barrier, n_cand * n_head - 1)
+
+    def ev_copy(off):
+        return pltpu.make_async_remote_copy(
+            src_ref=ev_ref, dst_ref=ev.at[head], send_sem=ev_send.at[off], recv_sem=ev_recv.at[head],
+            device_id=(me, (head + off) % n_head), device_id_type=MESH,
+        )
+
+    for off in range(1, n_head):
+        ev_copy(off).start()
+
+    def item_copy(off, t):
+        at = pl.ds(pl.multiple_of(t * TILE, TILE), TILE)
+        return pltpu.make_async_remote_copy(
+            src_ref=item_ref.at[at], dst_ref=feats.at[head, at],
+            send_sem=item_send.at[off * n_tiles + t], recv_sem=item_recv.at[head * n_tiles + t],
+            device_id=(me, (head + off) % n_head), device_id_type=MESH,
+        )
+
+    for t in range(n_tiles):
+        for off in range(1, n_head):
+            item_copy(off, t).start()
+
+    def tl_copy(c):
+        return pltpu.make_async_remote_copy(
+            src_ref=tl_ref, dst_ref=tl_all.at[me], send_sem=tl_send, recv_sem=tl_recv,
+            device_id=(c, head), device_id_type=MESH,
+        )
+
+    def send_list(off, carry):
+        tl_copy((me + off) % n_cand).start()
+        return carry
+
+    lax.fori_loop(1, n_cand, send_list, 0)
+    pltpu.make_async_copy(tl_ref, tl_all.at[me], tl_recv).start()
+
+    for off in range(1, n_head):
+        src = (head + off) % n_head
+        pltpu.make_async_copy(ev.at[src], ev.at[src], ev_recv.at[src]).wait()
+
+    for off in range(1, n_head):
+        add_half((head + off) % n_head)
+    pre, keys, values = sums
     keys = keys * (1.0 / math.sqrt(DH))
     values_t = values.T
     forget = pre[1]

time: 54.8 us -> 54.8 us (level)
  no operation moved by 1% of the time
where the time goes in v4:
time: 54.8 us; the launch traced here: 54.6 us
  Pallas kernels  51 us (93%)
  local copies, waits for them, and re-layouts  2.95 us (5%)
  between operations  0.65 us (1%)
    pallas_call x1, Pallas kernels, on_device(): pl.pallas_call(functools.partial(kernel, n_cand, n_head, users, events, h...  51 us
    unnamed x7, local copies, waits for them, and re-layouts  2.95 us

profile of v4, /device:TPU:1, one launch (start us, length us, event | category | flops | bytes accessed | tf_op | source)
XLA Modules:
  0.0 54.6 jit_solution(12968083202485805479)
XLA Ops:
  0.6 51.0 %shard_map.139 = (bf16[2,4,128,128]{3,2,1,0:T(8,128)(2,1)}, bf16[2,4,128]{2,1,0:T(4,128)(2,1)}, f32[2,512]{1,0:T(2,128)}) custom-call(bf16[128,512]{1,0:T(8,128)(2,1)} %bitcast.3, bf16[1024,512]{1,0:T(8,128)(2,1)} %item_ref.1, bf16[2,4,128,128]{3,2,1,0:T(8,128)(2,1)} %mem_ref.1, bf16[2,4,128]{2,1,0:T(4,128)(2,1)} %nrm_ref.1, bf16[1024,512]{1,0:T(8,128)(2,1)} %wq_ref.1, ...), custom_call_target="tpu_custom_call" | custom-call | tf_op jit(solution)/shard_map/pallas_call | solution.py:413
  51.7 0.0 copy-start.1
  51.7 1.7 %copy.18 = bf16[2,4,128,128]{3,2,1,0:T(8,128)(2,1)} copy(bf16[2,4,128,128]{3,2,1,0:T(8,128)(2,1)} %get-tuple-element.6) | data formatting | bytes 524288
  53.4 0.0 copy-done.1
  53.4 0.0 copy-start
  53.4 0.6 %copy.19 = bf16[2,4,128]{2,1,0:T(4,128)(2,1)} copy(bf16[2,4,128]{2,1,0:T(4,128)(2,1)S(1)} %copy-done.1) | data formatting | bytes 4096
  53.9 0.1 copy-done
  54.0 0.6 %copy.20 = f32[2,512]{1,0:T(2,128)} copy(f32[2,512]{1,0:T(2,128)S(1)} %copy-done) | data formatting | bytes 8192
Async XLA Ops:
  51.7 1.7 %copy-start.1 = (bf16[2,4,128]{2,1,0:T(4,128)(2,1)S(1)}, bf16[2,4,128]{2,1,0:T(4,128)(2,1)}, u32[]{:S(2)}) copy-start(bf16[2,4,128]{2,1,0:T(4,128)(2,1)} %get-tuple-element.7) | copy-start | bytes 6148
  53.4 0.7 %copy-start = (f32[2,512]{1,0:T(2,128)S(1)}, f32[2,512]{1,0:T(2,128)}, u32[]{:S(2)}) copy-start(f32[2,512]{1,0:T(2,128)} %get-tuple-element.8) | copy-start | bytes 12292
